TPU v7x, 256 devices: a whole 4x4x8 slice. The times are simulated.
256 devices in a mesh: seq: 32 (over x, y, core), head: 8 (over z).
Axes of the slice: x: 4, y: 4, z: 8, core: 2. Of those that a mesh axis runs over, the one named last changes fastest.
Arguments:
- queries: bfloat16 [262144, 1024], P('seq', 'head'), may hold values from -6 to 6
- keys: bfloat16 [262144, 1024], P('seq', 'head'), may hold values from -0.52734375 to 0.52734375
- values: bfloat16 [262144, 1024], P('seq', 'head'), may hold values from -6 to 6
- exponents: int32 [8], P('head'), may hold values from 16 to 4194304, as said below
- gain: float32 [1024], P('head'), may hold values from 0.1 to 1.9
Outputs:
- attended: bfloat16 [262144, 1024], P('seq', 'head')
- final_state: float32 [8, 128, 128], P(None, 'seq')
Inputs may be any that keep to these rules, and one draw needn't show every extreme that they name: `exponents`: each exponent is a power of two; some head has 16 and some head has 4194304.
All inputs are finite; a program needn't handle non-finite values.
Results may differ from a plain program's by a relative error of at most 0.0044.
Values sent between devices are 32-bit elements; how exact they have to be, the bound alone decides.
A program may use at most 64 MiB of HBM per device.

v0:
```python
import jax
import jax.numpy as jnp
from jax import lax
from jax.sharding import PartitionSpec as P

BLOCK = 256


def entering(value, axis, join, neutral):
    count, mine = (lax.axis_size(axis), lax.axis_index(axis))
    pieces = jax.tree.map(lambda part: lax.all_gather(part, axis), value)
    total = jax.tree.map(
        lambda part, zero: jnp.full_like(part, 0) + jnp.asarray(zero, part.dtype), value, neutral
    )

    def turn(position, total):
        longer = join(total, jax.tree.map(lambda part: part[position], pieces))
        return jax.tree.map(lambda new, old: jnp.where(position < mine, new, old), longer, total)

    return lax.fori_loop(0, count - 1, turn, total)


def broadcast(value, axis, source):
    kept = jnp.where(lax.axis_index(axis) == source, value, 0).astype(value.dtype)
    return lax.psum(kept, axis)


def on_device(queries, keys, values, exponents, gain):
    tok_rows, width = queries.shape
    heads_here = exponents.shape[0]
    head_dim = width // heads_here
    blocks = tok_rows // BLOCK
    rate = exponents.astype(jnp.float32) / 16777216.0
    qq = queries.reshape(blocks, BLOCK, heads_here, head_dim)
    kk = keys.reshape(blocks, BLOCK, heads_here, head_dim)
    vv = values.reshape(blocks, BLOCK, heads_here, head_dim)
    pos = jnp.arange(BLOCK).astype(jnp.float32)
    lower = pos[:, None] >= pos[None, :]
    gap = jnp.maximum(pos[:, None] - pos[None, :], 0.0)
    within = jnp.where(lower[None], jnp.exp2(-rate[:, None, None] * gap[None]), 0.0)
    scores = jnp.einsum("bihd,bjhd->bhij", qq, kk, preferred_element_type=jnp.float32)
    weights = (scores * within[None]).astype(jnp.bfloat16)
    local = jnp.einsum("bhij,bjhe->bihe", weights, vv, preferred_element_type=jnp.float32)
    tail = jnp.exp2(-rate[None, :] * (BLOCK - 1.0 - pos[:, None]))
    scaled = (kk.astype(jnp.float32) * tail[None, :, :, None]).astype(jnp.bfloat16)
    contrib = jnp.einsum("bjhd,bjhe->bhde", scaled, vv, preferred_element_type=jnp.float32)
    index_b = jnp.arange(blocks).astype(jnp.float32)
    steps_back = index_b[:, None] - 1.0 - index_b[None, :]
    chain = jnp.where(
        steps_back[None] >= 0.0,
        jnp.exp2(-rate[:, None, None] * BLOCK * jnp.maximum(steps_back, 0.0)[None]),
        0.0,
    )
    before = jnp.einsum("hbc,chde->bhde", chain, contrib, precision=lax.Precision.HIGHEST)
    ending_w = jnp.exp2(-rate[:, None] * BLOCK * (blocks - 1.0 - index_b[None, :]))
    own_total = jnp.einsum("hc,chde->hde", ending_w, contrib, precision=lax.Precision.HIGHEST)
    factor = jnp.exp2(-rate * tok_rows)
    count = lax.axis_size("seq")

    def combine(earlier, later):
        return (earlier[0] * later[0], later[0][:, None, None] * earlier[1] + later[1])

    identity = (jnp.ones_like(factor), jnp.zeros_like(own_total))
    prior = entering((factor, own_total), "seq", combine, identity)[1]
    inclusive = factor[:, None, None] * prior + own_total
    final_here = broadcast(inclusive, "seq", count - 1)
    offsets = jnp.exp2(-rate[None, :] * BLOCK * index_b[:, None])
    start_state = offsets[:, :, None, None] * prior[None] + before
    lead = jnp.exp2(-rate[None, :] * (pos[:, None] + 1.0))
    lifted = qq.astype(jnp.float32) * lead[None, :, :, None]
    inter = jnp.einsum("bihd,bhde->bihe", lifted, start_state, precision=lax.Precision.HIGHEST)
    raw = local + inter
    mean_sq = jnp.mean(raw * raw, axis=-1, keepdims=True)
    normed = raw * lax.rsqrt(mean_sq + 1e-06) * gain.reshape(heads_here, head_dim)
    attended = normed.astype(jnp.bfloat16).reshape(tok_rows, width)
    share = head_dim // count
    row_start = lax.axis_index("seq") * share
    own_rows = lax.dynamic_slice_in_dim(final_here, row_start, share, 1)
    final_state = lax.all_gather(own_rows, "head", axis=0, tiled=True)
    return (attended, final_state)


def solution(mesh):
    placed = (P("seq", "head"), P("seq", "head"), P("seq", "head"), P("head"), P("head"))
    return jax.shard_map(
        on_device,
        mesh=mesh,
        in_specs=placed,
        out_specs=(P("seq", "head"), P(None, "seq", None)),
        check_vma=False,
    )
```

profile of v0, /device:TPU:1, one launch (start us, length us, event | category | flops | bytes accessed | tf_op | source)
XLA Modules:
  0.0 300.0 jit_solution(8013491021424810727)
XLA Ops:
  9.3 4.1 %copy.12 = bf16[32,256,128]{1,2,0:T(8,128)(2,1)} copy(bf16[32,256,128]{2,1,0:T(8,128)(2,1)} %bitcast.60) | data formatting | bytes 4194304 | tf_op jit(solution)/shard_map/reshape.1
  13.4 2.3 fusion.13
  17.0 3.5 %fusion.18 = f32[1,128,128]{2,0,1:T(1,128)} fusion(f32[32,128,128]{2,1,0:T(8,128)S(1)} %fusion.13, f32[]{:T(128)} %bitcast.5), kind=kOutput, calls=%fused_computation.23 | convolution fusion | flops 6291584 | bytes 2162692 | tf_op jit(solution)/shard_map/hc,chde->hde/dot_general | solution.py:56
  21.8 65.4 %all-reduce = f32[32]{0:T(128)S(1)} all-reduce(f32[32]{0:T(128)S(1)} %fusion.47), channel_id=2, replica_groups=mesh['seq'=32,'head'=8] {'seq'}, use_global_device_ids=true, to_apply=%add | all-reduce | flops 32 | bytes 256
  89.4 6.5 %fusion.1 = f32[32,256,128]{2,1,0:T(8,128)} fusion(bf16[32,256,128]{2,1,0:T(8,128)(2,1)S(1)} %bitcast.56, f32[256,256]{1,0:T(8,128)S(1)} %exponential_select_fusion, bf16[32,256,128]{2,1,0:T(8,128)(2,1)} %bitcast.58, bf16[32,256,128]{2,1,0:T(8,128)(2,1)} %bitcast.61), kind=kOutput, calls=%fused_computation.4 | convolution fusion | flops 1077936128 | bytes 10747904 | tf_op jit(solution)/shard_map/bhij,bjhe->bihe/dot_general | solution.py:43
  96.0 69.5 %while.14 = (s32[]{:T(128)}, f32[1,128,128]{2,1,0:T(8,128)S(1)}, s32[]{:T(128)}, f32[32,1]{0,1:T(1,128)S(1)}, f32[32,1,128,128]{3,2,1,0:T(8,128)}, /*index=5*/s32[]{:T(128)}, s32[]{:T(128)}) while((s32[]{:T(128)}, f32[1,128,128]{2,1,0:T(8,128)S(1)}, s32[]{:T(128)}, f32[32,1]{0,1:T(1,128)S(1)}, f32[32,1,128,128]{3,2,1,0:T(8,128)}, ...), condition=%wide.region_1.2_spmd.clone, body=%wide.region_0.1_spmd.clone.sunk | while | flops 65540 | bytes 196733 | solution.py:20
  96.7 1.5 fusion.54
  98.9 1.5 fusion.54
  101.1 1.5 fusion.54
  103.4 1.5 fusion.54
  105.6 1.5 fusion.54
  107.8 1.5 fusion.54
  110.1 1.5 fusion.54
  112.3 1.5 fusion.54
  114.5 1.5 fusion.54
  116.8 1.5 fusion.54
  119.0 1.5 fusion.54
  121.2 1.5 fusion.54
  123.5 1.5 fusion.54
  125.7 1.5 fusion.54
  128.0 1.5 fusion.54
  130.2 1.5 fusion.54
  132.4 1.5 fusion.54
  134.7 1.5 fusion.54
  136.9 1.5 fusion.54
  139.1 1.5 fusion.54
  159.3 1.5 fusion.54
  166.8 5.8 %fusion.14 = f32[32,128,128]{2,0,1:T(8,128)S(1)} fusion(f32[32,128,128]{2,1,0:T(8,128)} %copy-done.1, f32[128,128]{1,0:T(8,128)S(1)} %bitcast.62, f32[32]{0:T(128)S(1)} %multiply_exponential_fusion.3, f32[]{:T(128)} %bitcast.5, f32[32]{0:T(128)S(1)} %iota_convert_fusion.1, f32[32]{0:T(128)S(1)} %broadcast_add_fusion), kind=kOutput, calls=%fused_computation.19 | convolution fusion | flops 202381312 | bytes 4260228 | tf_op jit(solution)/shard_map/hbc,chde->bhde/dot_general | solution.py:54
  172.6 8.3 %fusion.2 = (f32[32,256]{1,0:T(8,128)S(1)}, f32[32,128,256]{1,2,0:T(8,128)S(1)}) fusion(bf16[32,256,128]{2,1,0:T(8,128)(2,1)} %bitcast.59, f32[256]{0:T(256)S(1)} %multiply_exponential_fusion, f32[32,128,128]{2,0,1:T(8,128)S(1)} %fusion.14, f32[32,256,128]{2,1,0:T(8,128)S(1)} %copy-done.2), kind=kOutput, calls=%fused_computation.7 | convolution fusion | flops 1615847424 | bytes 12616704 | tf_op jit(solution)/shard_map/bihd,bhde->bihe/dot_general | solution.py:71
  180.9 2.2 fusion.4
  183.1 90.4 %all-reduce.3.cloned.1.call-done = f32[1,128,128]{2,1,0:T(8,128)} async-done(((f32[1,128,128]{2,1,0:T(8,128)}), f32[1,128,128]{2,1,0:T(8,128)}) %all-reduce.3.cloned.1.call-update) | async-done | bytes 65552 | tf_op jit(solution)/shard_map/psum | solution.py:25
  274.3 18.2 %all_gather.19 = f32[8,4,128]{2,1,0:T(4,128)S(1)} all-gather(f32[1,4,128]{2,1,0:T(4,128)S(1)} %constant_dynamic-slice_fusion.1), channel_id=1, replica_groups=mesh['seq'=32,'head'=8] {'head'}, dimensions={0}, use_global_device_ids=true | all-gather | bytes 18432 | tf_op jit(solution)/shard_map/all_gather | solution.py:79
  (74 shorter events, 44.8 us)
Async XLA Ops:
  7.2 6.2 %copy-start = (bf16[8192,128]{1,0:T(8,128)(2,1)S(1)}, bf16[8192,128]{1,0:T(8,128)(2,1)}, u32[]{:S(2)}) copy-start(bf16[8192,128]{1,0:T(8,128)(2,1)} %param.9) | copy-start | bytes 6291460
  7.2 88.8 %all-gather.4.cloned.1.call-start = ((), (), s32[]{:S(2)}) async-start(), calls=%async_computation.1 | async-start | bytes 2162688 | tf_op jit(solution)/shard_map/all_gather | solution.py:11
  15.7 1.3 copy-start.1
  15.7 4.9 %copy-start.5 = (u32[256]{0:T(256)S(1)}, u32[256]{0:T(256)}, u32[]{:S(2)}) copy-start(u32[256]{0:T(256)} %constant.78) | copy-start | bytes 3076
  20.5 253.1 %all-reduce.3.cloned.1.call-start = ((), (), s32[]{:S(2)}) async-start(), calls=%async_computation | async-start | bytes 131072 | tf_op jit(solution)/shard_map/psum | solution.py:25
  89.4 76.0 %copy-start.3 = (f32[1,128,128]{2,0,1:T(1,128)S(1)}, f32[1,128,128]{2,0,1:T(1,128)}, u32[]{:S(2)}) copy-start(f32[1,128,128]{2,0,1:T(1,128)} %fusion.18) | copy-start | bytes 196612
  166.8 5.8 %copy-start.2 = (f32[32,256,128]{2,1,0:T(8,128)S(1)}, f32[32,256,128]{2,1,0:T(8,128)}, u32[]{:S(2)}) copy-start(f32[32,256,128]{2,1,0:T(8,128)} %fusion.1) | copy-start | bytes 12582916
  172.5 8.4 %copy-start.4 = (f32[128]{0:T(128)S(1)}, f32[128]{0:T(128)}, u32[]{:S(2)}) copy-start(f32[128]{0:T(128)} %param.11) | copy-start | bytes 1540
Sparse Core Ops, SparseCore 0:
  20.6 53.1 all-gather.3
  166.9 106.6 all-reduce.2
where the time goes:
time: 306 us; the launch traced here: 300 us
  waiting for transfers between devices  90.5 us (30%)
  blocking collectives  83.6 us (27%)
  other arithmetic  55.6 us (18%)
  local copies, waits for them, and re-layouts  27.8 us (9%)
  matrix products  26.4 us (9%)
  between operations  15 us (5%)
    psum x1, waiting for transfers between devices, broadcast(): return lax.psum(kept, axis)  90.4 us
    unnamed x1, blocking collectives  65.4 us
    select_n x31, other arithmetic, turn(): jnp.where(position < mine, new, old)  48 us
    dynamic_slice x31, local copies, waits for them, and re-layouts, turn(): longer = join(total, jax.tree.map(lambda part: part[position], pieces))  20.6 us
    all_gather x1, blocking collectives, on_device(): final_state = lax.all_gather(own_rows, 'head', axis=0, tiled=True)  18.2 us
    dot_general x1, matrix products, on_device(): jnp.einsum('bihd,bhde->bihe', lifted, start_state, precision=lax.Precisio...  8.34 us
    dot_general x1, matrix products, on_device(): jnp.einsum('bhij,bjhe->bihe', weights, vv, preferred_element_type=jnp.flo...  6.55 us
  transfers between devices with their start and end apart: 2, of which 1 were waited for; matrix products, arithmetic and copies ran while one was open for 9% of the time, Pallas kernels for 0%

commit v1 on v0

v1 whole, which is shorter than its diff:
```python
import functools

import jax
import jax.numpy as jnp
from jax import lax
from jax.experimental import pallas as pl
from jax.experimental.pallas import tpu as pltpu
from jax.sharding import PartitionSpec as P

BLOCK = 256
PIECES = 8
FIRST = 12
MESH = pl.DeviceIdType.MESH
F32 = jnp.float32
BF16 = jnp.bfloat16


def rows(start, count):
    return pl.ds(pl.multiple_of(start, count), count)


def split(value):
    high = value.astype(BF16)
    return high, (value - high.astype(F32)).astype(BF16)


def state_kernel(
    n_seq, n_head,
    exps_hbm, gain_hbm, q_hbm, k_hbm, v_hbm,
    raw, q, prior, final, lead, gain, decay,
    k, v, exps, within, tail, before, own, gathered, prefix, landed, finals,
    in_sems, small_sems, send_sems, recv_sems,
):
    me, mine = lax.axis_index("seq"), lax.axis_index("head")
    tokens, width = q.shape
    blocks = tokens // BLOCK
    per_piece = blocks // PIECES
    piece_rows = per_piece * BLOCK

    def load(which, piece):
        src, dst = ((k_hbm, k), (v_hbm, v), (q_hbm, q))[which]
        part = rows(piece * piece_rows, piece_rows)
        return pltpu.make_async_copy(src.at[part], dst.at[part], in_sems.at[which, piece])

    read_exps = pltpu.make_async_copy(exps_hbm, exps, small_sems.at[0])
    read_gain = pltpu.make_async_copy(gain_hbm, gain, small_sems.at[1])
    read_exps.start()
    for piece in range(PIECES):
        load(0, piece).start()
        load(1, piece).start()
    for piece in range(PIECES):
        load(2, piece).start()
    read_gain.start()

    barrier = pltpu.get_barrier_semaphore()

    @pl.loop(1, n_seq)
    def _(step):
        pl.semaphore_signal(
            barrier, inc=1, device_id={"seq": lax.rem(me + step, n_seq)}, device_id_type=MESH
        )

    @pl.loop(1, n_head)
    def _(step):
        pl.semaphore_signal(
            barrier, inc=1, device_id={"head": lax.rem(mine + step, n_head)}, device_id_type=MESH
        )

    read_exps.wait()
    rate = exps[0].astype(F32) / 16777216.0
    row = lax.broadcasted_iota(jnp.int32, (BLOCK, width), 0).astype(F32)
    lead[...] = jnp.exp2(-rate * (row + 1.0))
    tail[...] = jnp.exp2(-rate * (BLOCK - 1.0 - row))
    gap = (
        lax.broadcasted_iota(jnp.int32, (BLOCK, BLOCK), 0)
        - lax.broadcasted_iota(jnp.int32, (BLOCK, BLOCK), 1)
    ).astype(F32)
    within[...] = jnp.where(gap >= 0.0, jnp.exp2(-rate * jnp.maximum(gap, 0.0)), 0.0)
    ones = jnp.ones((1, width), F32)
    decay[...] = jnp.exp2(-rate * BLOCK * ones)
    whole = jnp.exp2(-rate * tokens * ones)

    def contribute(piece, state):
        load(0, piece).wait()
        load(1, piece).wait()
        for j in range(per_piece):
            block = piece * per_piece + j
            part = rows(block * BLOCK, BLOCK)
            scaled = (k[part, :].astype(F32) * tail[...]).astype(BF16)
            term = lax.dot_general(
                scaled, v[part, :], (((0,), (0,)), ((), ())), preferred_element_type=F32
            )
            before[block] = state
            state = state * decay[...] + term
        return state

    total = lax.fori_loop(0, PIECES, contribute, jnp.zeros((width, width), F32))
    own[...] = total.reshape(own.shape)
    gathered[me] = own[me]
    pl.semaphore_wait(barrier, n_seq + n_head - 2)

    def exchange(src, dst, which, step):
        to = lax.rem(me + step, n_seq)
        return pltpu.make_async_remote_copy(
            src_ref=src.at[to], dst_ref=dst.at[me], send_sem=send_sems.at[which],
            recv_sem=recv_sems.at[which], device_id={"seq": to}, device_id_type=MESH,
        )

    def spread(step):
        return pltpu.make_async_remote_copy(
            src_ref=finals.at[mine], dst_ref=finals.at[mine], send_sem=send_sems.at[2],
            recv_sem=recv_sems.at[2], device_id={"head": lax.rem(mine + step, n_head)},
            device_id_type=MESH,
        )

    def arrived(dst, which, count):
        part = dst.at[pl.ds(0, count)]
        pltpu.make_async_copy(part, part, recv_sems.at[which]).wait()

    def left(src, which, count):
        part = src.at[pl.ds(0, count)]
        pltpu.make_async_copy(part, part, send_sems.at[which]).wait()

    @pl.loop(1, n_seq)
    def _(step):
        exchange(own, gathered, 0, step).start()

    def attend(block, carry):
        part = rows(block * BLOCK, BLOCK)
        queries, vals = q[part, :], v[part, :]
        scores = lax.dot_general(
            queries, k[part, :], (((1,), (1,)), ((), ())), preferred_element_type=F32
        )
        weights = (scores * within[...]).astype(BF16)
        local = jnp.dot(weights, vals, preferred_element_type=F32)
        inter = jnp.dot(
            jnp.concatenate([queries, queries], axis=1),
            jnp.concatenate(split(before[block]), axis=0),
            preferred_element_type=F32,
        )
        raw[part, :] = local + lead[...] * inter
        return carry

    @pl.loop(0, PIECES)
    def _(piece):
        load(2, piece).wait()

    first = blocks * FIRST // 32
    lax.fori_loop(0, first, attend, 0)

    arrived(gathered, 0, n_seq - 1)

    def advance(step, state):
        prefix[step] = state
        return state * whole + gathered[step]

    finals[mine] = lax.fori_loop(
        0, n_seq, advance, jnp.zeros(gathered.shape[1:], F32)
    )
    landed[me] = prefix[me]

    @pl.loop(1, n_seq)
    def _(step):
        exchange(prefix, landed, 1, step).start()

    @pl.loop(1, n_head)
    def _(step):
        spread(step).start()

    lax.fori_loop(first, blocks, attend, 0)

    read_gain.wait()
    arrived(finals, 2, n_head - 1)
    final[...] = finals[...]
    arrived(landed, 1, n_seq - 1)
    high, low = split(landed[...].reshape(width, width))
    prior[:width, :] = high
    prior[width:, :] = low
    left(own, 0, n_seq - 1)
    left(prefix, 1, n_seq - 1)
    left(finals, 2, n_head - 1)


def finish_kernel(
    raw, q, prior, final, lead, gain, decay, out_hbm, final_out, out, sems, final_sem
):
    tokens, width = q.shape
    blocks = tokens // BLOCK
    per_piece = blocks // PIECES
    piece_rows = per_piece * BLOCK

    def write(piece):
        part = rows(piece * piece_rows, piece_rows)
        return pltpu.make_async_copy(out.at[part], out_hbm.at[part], sems.at[piece])

    write_final = pltpu.make_async_copy(final, final_out, final_sem.at[0])
    write_final.start()

    def finish(piece, ahead):
        for j in range(per_piece):
            part = rows((piece * per_piece + j) * BLOCK, BLOCK)
            queries = q[part, :]
            inter = jnp.dot(
                jnp.concatenate([queries, queries], axis=1), prior[...], preferred_element_type=F32
            )
            value = raw[part, :] + (lead[...] * ahead) * inter
            mean_sq = jnp.mean(value * value, axis=-1, keepdims=True)
            out[part, :] = (value * lax.rsqrt(mean_sq + 1e-06) * gain[...]).astype(BF16)
            ahead = ahead * decay[...]
        write(piece).start()
        return ahead

    lax.fori_loop(0, PIECES, finish, jnp.ones((1, width), F32))

    @pl.loop(0, PIECES)
    def _(piece):
        write(piece).wait()

    write_final.wait()


def on_device(n_seq, n_head, queries, keys, values, exponents, gain):
    tokens, width = queries.shape
    share = width // n_seq
    vmem = pl.BlockSpec(memory_space=pltpu.VMEM)
    anywhere = pl.BlockSpec(memory_space=pl.ANY)
    hbm = pl.BlockSpec(memory_space=pltpu.HBM)
    blocks = tokens // BLOCK
    kept = pl.pallas_call(
        functools.partial(state_kernel, n_seq, n_head),
        out_shape=(
            pltpu.VMEM((tokens, width), F32),
            pltpu.VMEM((tokens, width), BF16),
            pltpu.VMEM((2 * width, width), BF16),
            pltpu.VMEM((n_head, share, width), F32),
            pltpu.VMEM((BLOCK, width), F32),
            pltpu.VMEM((1, width), F32),
            pltpu.VMEM((1, width), F32),
        ),
        in_specs=[anywhere] + [hbm] * 4,
        out_specs=(vmem,) * 7,
        scratch_shapes=[
            pltpu.VMEM((tokens, width), BF16),
            pltpu.VMEM((tokens, width), BF16),
            pltpu.SMEM((1,), jnp.int32),
            pltpu.VMEM((BLOCK, BLOCK), F32),
            pltpu.VMEM((BLOCK, width), F32),
            pltpu.VMEM((blocks, width, width), F32),
            pltpu.VMEM((n_seq, share, width), F32),
            pltpu.VMEM((n_seq, share, width), F32),
            pltpu.VMEM((n_seq, share, width), F32),
            pltpu.VMEM((n_seq, share, width), F32),
            pltpu.VMEM((n_head, share, width), F32),
            pltpu.SemaphoreType.DMA((3, PIECES)),
            pltpu.SemaphoreType.DMA((2,)),
            pltpu.SemaphoreType.DMA((3,)),
            pltpu.SemaphoreType.DMA((3,)),
        ],
        compiler_params=pltpu.CompilerParams(
            collective_id=0, has_side_effects=True, vmem_limit_bytes=32 * 1024 * 1024
        ),
        name="state",
    )(exponents, *(
        pltpu.with_memory_space_constraint(array, pltpu.HBM)
        for array in (gain.reshape(1, width), queries, keys, values)
    ))
    return pl.pallas_call(
        finish_kernel,
        out_shape=(
            jax.ShapeDtypeStruct((tokens, width), BF16),
            jax.ShapeDtypeStruct((n_head, share, width), F32),
        ),
        in_specs=[vmem] * 7,
        out_specs=(anywhere, anywhere),
        scratch_shapes=[
            pltpu.VMEM((tokens, width), BF16),
            pltpu.SemaphoreType.DMA((PIECES,)),
            pltpu.SemaphoreType.DMA((1,)),
        ],
        compiler_params=pltpu.CompilerParams(vmem_limit_bytes=32 * 1024 * 1024),
        name="finish",
    )(*kept)


def solution(mesh):
    return jax.shard_map(
        functools.partial(on_device, mesh.shape["seq"], mesh.shape["head"]),
        mesh=mesh,
        in_specs=(P("seq", "head"), P("seq", "head"), P("seq", "head"), P("head"), P("head")),
        out_specs=(P("seq", "head"), P(None, "seq", None)),
        check_vma=False,
    )
```

time: 306 us -> 29.7 us (0.10); the launches traced: 300 us -> 29.6 us
  waiting for transfers between devices: 90.5 us -> 0 us
  blocking collectives: 83.6 us -> 0 us
  other arithmetic: 55.6 us -> 0 us
  Pallas kernels: 0 us -> 28.4 us
  local copies, waits for them, and re-layouts: 27.8 us -> 0 us
  matrix products: 26.4 us -> 0 us
  between operations: 15 us -> 1.28 us
    psum x1 -> x0, waiting for transfers between devices: 90.4 us -> none  [broadcast(): return lax.psum(kept, axis)]
    unnamed x1 -> x0, blocking collectives: 65.4 us -> none
    select_n x33 -> x0, other arithmetic: 50.1 us -> none  [the longest x31 48 us: turn(): jnp.where(position < mine, new, old)]
    pallas_call x0 -> x2, Pallas kernels: none -> 28.4 us  [the longest x1 24.5 us: on_device(): pl.pallas_call(functools.partial(state_kernel, n_seq, n_head), out_shape=...]
    dot_general x5 -> x0, matrix products: 26.4 us -> none  [the longest x1 8.34 us: on_device(): jnp.einsum('bihd,bhde->bihe', lifted, start_state, precision=lax.Precisio...]
    dynamic_slice x32 -> x0, local copies, waits for them, and re-layouts: 21.2 us -> none  [the longest x31 20.6 us: turn(): longer = join(total, jax.tree.map(lambda part: part[position], pieces))]
    all_gather x1 -> x0, blocking collectives: 18.2 us -> none  [on_device(): final_state = lax.all_gather(own_rows, 'head', axis=0, tiled=True)]
    another operation x1 -> x0, local copies, waits for them, and re-layouts: 4.07 us -> none
  transfers between devices with their start and end apart: 2 -> 0, of which waited for: 1 -> 0; matrix products, arithmetic and copies ran while one was open for 9% -> 0% of each run, Pallas kernels for 0% -> 0%
where the time goes in v1:
time: 29.7 us; the launch traced here: 29.6 us
  Pallas kernels  28.4 us (96%)
  between operations  1.28 us (4%)
    pallas_call x1, Pallas kernels, on_device(): pl.pallas_call(functools.partial(state_kernel, n_seq, n_head), out_shape=...  24.5 us
    pallas_call x1, Pallas kernels, on_device(): pl.pallas_call(finish_kernel, out_shape=(jax.ShapeDtypeStruct((tokens, wi...  3.89 us

profile of v1, /device:TPU:1, one launch (start us, length us, event | category | flops | bytes accessed | tf_op | source)
XLA Modules:
  0.0 29.6 jit_solution(4548399206870879421)
XLA Ops:
  1.3 24.5 %state.1 = (f32[8192,128]{1,0:T(8,128)S(1)}, bf16[8192,128]{1,0:T(8,128)(2,1)S(1)}, bf16[256,128]{1,0:T(8,128)(2,1)S(1)}, f32[8,4,128]{2,1,0:T(4,128)S(1)}, f32[...) custom-call(s32[1]{0:T(128)S(6)} %copy.7.exps_hbm, f32[1,128]{1,0:T(1,128)} %bitcast.1, ...), custom_call_target="tpu_custom_call" | custom-call | tf_op jit(solution)/shard_map/state/pallas_call | solution.py:229
  25.8 3.9 %finish.1 = (bf16[8192,128]{1,0:T(8,128)(2,1)}, f32[8,4,128]{2,1,0:T(4,128)}) custom-call(f32[8192,128]{1,0:T(8,128)S(1)} %get-tuple-element.9.raw, bf16[8192,128]{1,0:T(8,128)(2,1)S(1)} %get-tuple-element.10.q, bf16[256,128]{1,0:T(8,128)(2,1)S(1)} %get-tuple-element.11.prior, f32[8,4,128]{2,1,0:T(4,128)S(1)} %get-tuple-element.12.final, ...), custom_call_target="tpu_custom_call" | custom-call | tf_op jit(solution)/shard_map/finish/pallas_call | solution.py:267

commit v2 on v1

v2 whole, which is shorter than its diff:
```python
import functools

import jax
import jax.numpy as jnp
from jax import lax
from jax.experimental import pallas as pl
from jax.experimental.pallas import tpu as pltpu
from jax.sharding import PartitionSpec as P

BLOCK = 256
PIECES = 4
MESH = pl.DeviceIdType.MESH
F32 = jnp.float32
BF16 = jnp.bfloat16


def rows(start, count):
    return pl.ds(pl.multiple_of(start, count), count)


def split(value):
    high = value.astype(BF16)
    return high, (value - high.astype(F32)).astype(BF16)


def state_kernel(
    n_seq, n_head,
    exps_hbm, gain_hbm, q_hbm, k_hbm, v_hbm,
    out, final,
    q, k, v, raw, exps, gain, within, lead, tail, before, own, gathered, prefix, landed,
    last, finals, in_sems, small_sems, send_sems, recv_sems, ready,
):
    me, mine = lax.axis_index("seq"), lax.axis_index("head")
    n_hubs = n_seq // 2
    half = n_hubs // 2
    ring = min(4, half)
    is_hub = me < n_hubs
    hub_count = is_hub.astype(jnp.int32)
    my_chip = me // 2
    my_hub = 2 * lax.rem(my_chip, half) + my_chip // half
    chip = jnp.minimum(me // 2 + half * lax.rem(me, 2), n_hubs - 1)
    tokens, width = q.shape
    blocks = tokens // BLOCK
    per_piece = blocks // PIECES
    piece_rows = per_piece * BLOCK

    def load(which, piece):
        src, dst = ((k_hbm, k), (v_hbm, v), (q_hbm, q))[which]
        part = rows(piece * piece_rows, piece_rows)
        return pltpu.make_async_copy(src.at[part], dst.at[part], in_sems.at[which, piece])

    read_exps = pltpu.make_async_copy(exps_hbm, exps, small_sems.at[0])
    read_gain = pltpu.make_async_copy(gain_hbm, gain, small_sems.at[1])
    read_exps.start()
    for piece in range(PIECES):
        load(0, piece).start()
        load(1, piece).start()
    read_gain.start()

    barrier = pltpu.get_barrier_semaphore()

    def signal(sem, seq, head):
        pl.semaphore_signal(
            sem, inc=1, device_id={"seq": seq, "head": head}, device_id_type=MESH
        )

    @pl.when(is_hub)
    def _():
        @pl.loop(1, n_seq)
        def _(step):
            signal(barrier, lax.rem(me + step, n_seq), mine)

        @pl.loop(mine + 1, n_head)
        def _(head):
            signal(barrier, 2 * chip, head)
            signal(barrier, 2 * chip + 1, head)

    @pl.loop(mine + 1, n_head)
    def _(head):
        signal(barrier, my_hub, head)

    read_exps.wait()
    rate = exps[0].astype(F32) / 16777216.0
    row = lax.broadcasted_iota(jnp.int32, (BLOCK, width), 0).astype(F32)
    lead[...] = jnp.exp2(-rate * (row + 1.0))
    tail[...] = jnp.exp2(-rate * (BLOCK - 1.0 - row))
    gap = (
        lax.broadcasted_iota(jnp.int32, (BLOCK, BLOCK), 0)
        - lax.broadcasted_iota(jnp.int32, (BLOCK, BLOCK), 1)
    ).astype(F32)
    within[...] = jnp.where(gap >= 0.0, jnp.exp2(-rate * jnp.maximum(gap, 0.0)), 0.0)
    ones = jnp.ones((1, width), F32)
    decay = jnp.exp2(-rate * BLOCK * ones)
    whole = jnp.exp2(-rate * tokens * ones)

    def contribute(piece, state):
        load(0, piece).wait()
        load(1, piece).wait()
        for j in range(per_piece):
            block = piece * per_piece + j
            part = rows(block * BLOCK, BLOCK)
            scaled = (k[part, :].astype(F32) * tail[...]).astype(BF16)
            term = lax.dot_general(
                scaled, v[part, :], (((0,), (0,)), ((), ())), preferred_element_type=F32
            )
            before[block] = state
            state = state * decay + term
        return state

    total = lax.fori_loop(0, PIECES, contribute, jnp.zeros((width, width), F32))
    own[...] = total.reshape(own.shape)
    for piece in range(PIECES):
        load(2, piece).start()

    pl.semaphore_wait(barrier, n_hubs - hub_count + mine * (1 + 2 * hub_count))

    def contribution(to, to_chip):
        return pltpu.make_async_remote_copy(
            src_ref=own.at[to_chip], dst_ref=gathered.at[me], send_sem=send_sems.at[0],
            recv_sem=recv_sems.at[0], device_id={"seq": to, "head": mine}, device_id_type=MESH,
        )

    def entering(to):
        return pltpu.make_async_remote_copy(
            src_ref=prefix.at[to], dst_ref=landed.at[chip], send_sem=send_sems.at[1],
            recv_sem=recv_sems.at[1], device_id={"seq": to, "head": mine}, device_id_type=MESH,
        )

    def ending(core, head):
        return pltpu.make_async_remote_copy(
            src_ref=last.at[core], dst_ref=finals.at[mine], send_sem=send_sems.at[2],
            recv_sem=recv_sems.at[2], device_id={"seq": 2 * chip + core, "head": head},
            device_id_type=MESH,
        )

    def drain(sem, ref, count):
        part = ref.at[pl.ds(0, count)]
        pltpu.make_async_copy(part, part, sem).wait()

    across = lax.rem(my_chip, ring)
    for offset in sorted(range(ring), key=lambda d: -min(d, ring - d)):
        for start in range(0, half, ring):
            for core in range(2):
                spot = start + lax.rem(across + offset, ring)
                to = 2 * spot + core

                @pl.when(to != me)
                def _():
                    contribution(to, spot + half * core).start()

    @pl.loop(0, mine)
    def _(head):
        signal(ready, my_hub, head)

    def attend(block, carry):
        part = rows(block * BLOCK, BLOCK)
        queries, vals = q[part, :], v[part, :]
        scores = lax.dot_general(
            queries, k[part, :], (((1,), (1,)), ((), ())), preferred_element_type=F32
        )
        weights = (scores * within[...]).astype(BF16)
        local = jnp.dot(weights, vals, preferred_element_type=F32)
        inter = jnp.dot(
            jnp.concatenate([queries, queries], axis=1),
            jnp.concatenate(split(before[block]), axis=0),
            preferred_element_type=F32,
        )
        raw[part, :] = local + lead[...] * inter
        return carry

    for piece in range(PIECES):
        load(2, piece).wait()
    first = blocks * 3 // 4
    lax.fori_loop(0, first, attend, 0, unroll=min(8, first))

    @pl.when(is_hub)
    def _():
        gathered[me] = own[chip]
        drain(recv_sems.at[0], gathered, n_seq - 1)
        state = jnp.zeros(gathered.shape[1:], F32)
        for step in range(n_seq):
            prefix[step] = state
            state = state * whole + gathered[step]
        last[...] = state.reshape(last.shape)

        @pl.when(2 * chip == me)
        def _():
            finals[mine] = last[0]

        @pl.loop(0, mine)
        def _(head):
            ending(0, head).start()
            ending(1, head).start()

        @pl.when(2 * chip != me)
        def _():
            ending(0, mine).start()

        ending(1, mine).start()
        landed[chip] = prefix[me]

        @pl.loop(1, n_hubs)
        def _(step):
            entering(lax.rem(me + step, n_hubs)).start()

        @pl.loop(0, n_hubs)
        def _(step):
            entering(n_hubs + lax.rem(me + step, n_hubs)).start()

        @pl.when(mine < n_head - 1)
        def _():
            pl.semaphore_wait(ready, 2 * (n_head - 1 - mine))

        @pl.loop(mine + 1, n_head)
        def _(head):
            ending(0, head).start()
            ending(1, head).start()

    lax.fori_loop(first, blocks, attend, 0, unroll=min(8, blocks - first))
    read_gain.wait()

    @pl.when(is_hub)
    def _():
        drain(recv_sems.at[1], landed, n_hubs - 1)

    @pl.when(jnp.logical_not(is_hub))
    def _():
        drain(recv_sems.at[1], landed, n_hubs)

    prior = jnp.concatenate(split(landed[...].reshape(width, width)), axis=0)

    def finish(piece, ahead):
        for j in range(per_piece):
            part = rows((piece * per_piece + j) * BLOCK, BLOCK)
            queries = q[part, :]
            inter = jnp.dot(
                jnp.concatenate([queries, queries], axis=1), prior, preferred_element_type=F32
            )
            value = raw[part, :] + (lead[...] * ahead) * inter
            mean_sq = jnp.mean(value * value, axis=-1, keepdims=True)
            out[part, :] = (value * lax.rsqrt(mean_sq + 1e-06) * gain[...]).astype(BF16)
            ahead = ahead * decay
        return ahead

    lax.fori_loop(0, PIECES, finish, ones)

    @pl.when(is_hub)
    def _():
        drain(send_sems.at[0], own, n_hubs - 1)
        drain(send_sems.at[1], prefix, n_seq - 1)

        @pl.when(2 * chip == me)
        def _():
            drain(send_sems.at[2], finals.at[pl.ds(0, n_head - 1)], n_head - 1)

        @pl.when(2 * chip != me)
        def _():
            drain(send_sems.at[2], finals, n_head)

        drain(send_sems.at[2], finals, n_head)

    @pl.when(jnp.logical_not(is_hub))
    def _():
        drain(send_sems.at[0], own, n_hubs)

    @pl.when(my_hub == me)
    def _():
        drain(recv_sems.at[2], finals, n_head - 1)

    @pl.when(my_hub != me)
    def _():
        drain(recv_sems.at[2], finals, n_head)

    final[...] = finals[...]


def write_kernel(out, final, out_hbm, final_hbm, sems):
    piece_rows = out.shape[0] // PIECES
    copies = [pltpu.make_async_copy(final, final_hbm, sems.at[PIECES])]
    for piece in range(PIECES):
        part = pl.ds(piece * piece_rows, piece_rows)
        copies.append(pltpu.make_async_copy(out.at[part], out_hbm.at[part], sems.at[piece]))
    for copy in copies:
        copy.start()
    for copy in copies:
        copy.wait()


def on_device(n_seq, n_head, queries, keys, values, exponents, gain):
    tokens, width = queries.shape
    share = width // n_seq
    n_hubs = n_seq // 2
    vmem = pl.BlockSpec(memory_space=pltpu.VMEM)
    anywhere = pl.BlockSpec(memory_space=pl.ANY)
    hbm = pl.BlockSpec(memory_space=pltpu.HBM)
    blocks = tokens // BLOCK
    kept = pl.pallas_call(
        functools.partial(state_kernel, n_seq, n_head),
        out_shape=(
            pltpu.VMEM((tokens, width), BF16),
            pltpu.VMEM((n_head, share, width), F32),
        ),
        in_specs=[anywhere] + [hbm] * 4,
        out_specs=(vmem,) * 2,
        scratch_shapes=[
            pltpu.VMEM((tokens, width), BF16),
            pltpu.VMEM((tokens, width), BF16),
            pltpu.VMEM((tokens, width), BF16),
            pltpu.VMEM((tokens, width), F32),
            pltpu.SMEM((1,), jnp.int32),
            pltpu.VMEM((1, width), F32),
            pltpu.VMEM((BLOCK, BLOCK), F32),
            pltpu.VMEM((BLOCK, width), F32),
            pltpu.VMEM((BLOCK, width), F32),
            pltpu.VMEM((blocks, width, width), F32),
            pltpu.VMEM((n_hubs, 2 * share, width), F32),
            pltpu.VMEM((n_seq, 2 * share, width), F32),
            pltpu.VMEM((n_seq, 2 * share, width), F32),
            pltpu.VMEM((n_hubs, 2 * share, width), F32),
            pltpu.VMEM((2, share, width), F32),
            pltpu.VMEM((n_head, share, width), F32),
            pltpu.SemaphoreType.DMA((3, PIECES)),
            pltpu.SemaphoreType.DMA((2,)),
            pltpu.SemaphoreType.DMA((3,)),
            pltpu.SemaphoreType.DMA((3,)),
            pltpu.SemaphoreType.REGULAR,
        ],
        compiler_params=pltpu.CompilerParams(
            collective_id=0, has_side_effects=True, vmem_limit_bytes=40 * 1024 * 1024
        ),
        name="state",
    )(exponents, *(
        pltpu.with_memory_space_constraint(array, pltpu.HBM)
        for array in (gain.reshape(1, width), queries, keys, values)
    ))
    return pl.pallas_call(
        write_kernel,
        out_shape=(
            jax.ShapeDtypeStruct((tokens, width), BF16),
            jax.ShapeDtypeStruct((n_head, share, width), F32),
        ),
        in_specs=[vmem] * 2,
        out_specs=(anywhere, anywhere),
        scratch_shapes=[pltpu.SemaphoreType.DMA((PIECES + 1,))],
        compiler_params=pltpu.CompilerParams(vmem_limit_bytes=32 * 1024 * 1024),
        name="write",
    )(*kept)


def solution(mesh):
    return jax.shard_map(
        functools.partial(on_device, mesh.shape["seq"], mesh.shape["head"]),
        mesh=mesh,
        in_specs=(P("seq", "head"), P("seq", "head"), P("seq", "head"), P("head"), P("head")),
        out_specs=(P("seq", "head"), P(None, "seq", None)),
        check_vma=False,
    )
```

time: 29.7 us -> 22.8 us (0.77)
  Pallas kernels: 28.4 us -> 21.4 us
    pallas_call x1, Pallas kernels: 24.5 us -> 20 us  [on_device(): pl.pallas_call(functools.partial(state_kernel, n_seq, n_head), out_shape=...]
    pallas_call x1, Pallas kernels: 3.89 us -> 1.36 us  [on_device(): pl.pallas_call(write_kernel, out_shape=(jax.ShapeDtypeStruct((tokens, wid...]
where the time goes in v2:
time: 22.8 us; the launch traced here: 22.7 us
  Pallas kernels  21.4 us (94%)
  between operations  1.29 us (6%)
    pallas_call x1, Pallas kernels, on_device(): pl.pallas_call(functools.partial(state_kernel, n_seq, n_head), out_shape=...  20 us
    pallas_call x1, Pallas kernels, on_device(): pl.pallas_call(write_kernel, out_shape=(jax.ShapeDtypeStruct((tokens, wid...  1.36 us

profile of v2, /device:TPU:1, one launch (start us, length us, event | category | flops | bytes accessed | tf_op | source)
XLA Modules:
  0.0 22.7 jit_solution(8898812343917109668)
XLA Ops:
  1.3 20.0 %state.1 = (bf16[8192,128]{1,0:T(8,128)(2,1)S(1)}, f32[8,4,128]{2,1,0:T(4,128)S(1)}) custom-call(s32[1]{0:T(128)S(6)} %copy.7.exps_hbm, f32[1,128]{1,0:T(1,128)} %bitcast.1, bf16[8192,128]{1,0:T(8,128)(2,1)} %q_hbm.1, bf16[8192,128]{1,0:T(8,128)(2,1)} %k_hbm.1, bf16[8192,128]{1,0:T(8,128)(2,1)} %v_hbm.1), custom_call_target="tpu_custom_call" | custom-call | tf_op jit(solution)/shard_map/state/pallas_call | solution.py:297
  21.3 1.4 %write.1 = (bf16[8192,128]{1,0:T(8,128)(2,1)}, f32[8,4,128]{2,1,0:T(4,128)}) custom-call(bf16[8192,128]{1,0:T(8,128)(2,1)S(1)} %get-tuple-element.4.out, f32[8,4,128]{2,1,0:T(4,128)S(1)} %get-tuple-element.5.final), custom_call_target="tpu_custom_call" | custom-call | tf_op jit(solution)/shard_map/write/pallas_call | solution.py:336

commit v3 on v2

--- a/solution.py
+++ b/solution.py
@@ -9,6 +9,7 @@
 
 BLOCK = 256
 PIECES = 4
+EARLY = 1
 MESH = pl.DeviceIdType.MESH
 F32 = jnp.float32
 BF16 = jnp.bfloat16
@@ -28,7 +29,7 @@
     exps_hbm, gain_hbm, q_hbm, k_hbm, v_hbm,
     out, final,
     q, k, v, raw, exps, gain, within, lead, tail, before, own, gathered, prefix, landed,
-    last, finals, in_sems, small_sems, send_sems, recv_sems, ready,
+    last, finals, toward, direct, in_sems, small_sems, send_sems, recv_sems, ready,
 ):
     me, mine = lax.axis_index("seq"), lax.axis_index("head")
     n_hubs = n_seq // 2
@@ -41,12 +42,17 @@
     chip = jnp.minimum(me // 2 + half * lax.rem(me, 2), n_hubs - 1)
     tokens, width = q.shape
     blocks = tokens // BLOCK
-    per_piece = blocks // PIECES
-    piece_rows = per_piece * BLOCK
+    cuts = [blocks * part // 16 for part in (0, 5, 10, 14, 16)]
+    share = width // n_seq
+    far = n_head // 2
+    is_far = mine >= far
+    is_early = jnp.logical_and(me == EARLY, mine == 0)
+
+    skip = jnp.logical_and(chip == EARLY // 2, is_far)
 
     def load(which, piece):
         src, dst = ((k_hbm, k), (v_hbm, v), (q_hbm, q))[which]
-        part = rows(piece * piece_rows, piece_rows)
+        part = pl.ds(cuts[piece] * BLOCK, (cuts[piece + 1] - cuts[piece]) * BLOCK)
         return pltpu.make_async_copy(src.at[part], dst.at[part], in_sems.at[which, piece])
 
     read_exps = pltpu.make_async_copy(exps_hbm, exps, small_sems.at[0])
@@ -79,59 +85,69 @@
     def _(head):
         signal(barrier, my_hub, head)
 
+    @pl.when(is_early)
+    def _():
+        @pl.loop(far, n_head)
+        def _(head):
+            @pl.loop(0, n_seq)
+            def _(seq):
+                signal(barrier, seq, head)
+
     read_exps.wait()
     rate = exps[0].astype(F32) / 16777216.0
     row = lax.broadcasted_iota(jnp.int32, (BLOCK, width), 0).astype(F32)
-    lead[...] = jnp.exp2(-rate * (row + 1.0))
     tail[...] = jnp.exp2(-rate * (BLOCK - 1.0 - row))
-    gap = (
-        lax.broadcasted_iota(jnp.int32, (BLOCK, BLOCK), 0)
-        - lax.broadcasted_iota(jnp.int32, (BLOCK, BLOCK), 1)
-    ).astype(F32)
-    within[...] = jnp.where(gap >= 0.0, jnp.exp2(-rate * jnp.maximum(gap, 0.0)), 0.0)
     ones = jnp.ones((1, width), F32)
     decay = jnp.exp2(-rate * BLOCK * ones)
     whole = jnp.exp2(-rate * tokens * ones)
 
-    def contribute(piece, state):
+    total = jnp.zeros((width, width), F32)
+    for piece in range(PIECES):
         load(0, piece).wait()
         load(1, piece).wait()
-        for j in range(per_piece):
-            block = piece * per_piece + j
-            part = rows(block * BLOCK, BLOCK)
+        for block in range(cuts[piece], cuts[piece + 1]):
+            part = pl.ds(block * BLOCK, BLOCK)
             scaled = (k[part, :].astype(F32) * tail[...]).astype(BF16)
             term = lax.dot_general(
                 scaled, v[part, :], (((0,), (0,)), ((), ())), preferred_element_type=F32
             )
-            before[block] = state
-            state = state * decay + term
-        return state
-
-    total = lax.fori_loop(0, PIECES, contribute, jnp.zeros((width, width), F32))
+            before[block] = total
+            total = total * decay + term
     own[...] = total.reshape(own.shape)
-    for piece in range(PIECES):
-        load(2, piece).start()
-
-    pl.semaphore_wait(barrier, n_hubs - hub_count + mine * (1 + 2 * hub_count))
+    left = (n_seq - 1 - me).astype(F32) * tokens
+    toward[...] = total[EARLY * share:(EARLY + 1) * share, :] * jnp.exp2(-rate * left * ones)
+
+    pl.semaphore_wait(
+        barrier, n_hubs - hub_count + mine * (1 + 2 * hub_count) + is_far.astype(jnp.int32)
+    )
 
     def contribution(to, to_chip):
         return pltpu.make_async_remote_copy(
             src_ref=own.at[to_chip], dst_ref=gathered.at[me], send_sem=send_sems.at[0],
-            recv_sem=recv_sems.at[0], device_id={"seq": to, "head": mine}, device_id_type=MESH,
+            recv_sem=recv_sems.at[hub_count], device_id={"seq": to, "head": mine}, device_id_type=MESH,
         )
 
     def entering(to):
         return pltpu.make_async_remote_copy(
             src_ref=prefix.at[to], dst_ref=landed.at[chip], send_sem=send_sems.at[1],
-            recv_sem=recv_sems.at[1], device_id={"seq": to, "head": mine}, device_id_type=MESH,
+            recv_sem=recv_sems.at[2], device_id={"seq": to, "head": mine}, device_id_type=MESH,
         )
 
     def ending(core, head):
         return pltpu.make_async_remote_copy(
             src_ref=last.at[core], dst_ref=finals.at[mine], send_sem=send_sems.at[2],
-            recv_sem=recv_sems.at[2], device_id={"seq": 2 * chip + core, "head": head},
+            recv_sem=recv_sems.at[3], device_id={"seq": 2 * chip + core, "head": head},
             device_id_type=MESH,
         )
+
+    to_early = pltpu.make_async_remote_copy(
+        src_ref=toward, dst_ref=direct.at[jnp.maximum(mine - far, 0), me], send_sem=send_sems.at[3],
+        recv_sem=recv_sems.at[4], device_id={"seq": EARLY, "head": 0}, device_id_type=MESH,
+    )
+
+    @pl.when(is_far)
+    def _():
+        to_early.start()
 
     def drain(sem, ref, count):
         part = ref.at[pl.ds(0, count)]
@@ -152,6 +168,15 @@
     def _(head):
         signal(ready, my_hub, head)
 
+    for piece in range(PIECES):
+        load(2, piece).start()
+    lead[...] = jnp.exp2(-rate * (row + 1.0))
+    gap = (
+        lax.broadcasted_iota(jnp.int32, (BLOCK, BLOCK), 0)
+        - lax.broadcasted_iota(jnp.int32, (BLOCK, BLOCK), 1)
+    ).astype(F32)
+    within[...] = jnp.where(gap >= 0.0, jnp.exp2(-rate * jnp.maximum(gap, 0.0)), 0.0)
+
     def attend(block, carry):
         part = rows(block * BLOCK, BLOCK)
         queries, vals = q[part, :], v[part, :]
@@ -176,9 +201,11 @@
     @pl.when(is_hub)
     def _():
         gathered[me] = own[chip]
-        drain(recv_sems.at[0], gathered, n_seq - 1)
+        drain(recv_sems.at[1], gathered, n_hubs - 1)
         state = jnp.zeros(gathered.shape[1:], F32)
         for step in range(n_seq):
+            if step == n_hubs:
+                drain(recv_sems.at[0], gathered, n_seq - n_hubs)
             prefix[step] = state
             state = state * whole + gathered[step]
         last[...] = state.reshape(last.shape)
@@ -189,8 +216,11 @@
 
         @pl.loop(0, mine)
         def _(head):
-            ending(0, head).start()
-            ending(1, head).start()
+            @pl.when(jnp.logical_not(jnp.logical_and(skip, head == 0)))
+            def _():
+                ending(EARLY % 2, head).start()
+
+            ending(1 - EARLY % 2, head).start()
 
         @pl.when(2 * chip != me)
         def _():
@@ -221,17 +251,17 @@
 
     @pl.when(is_hub)
     def _():
-        drain(recv_sems.at[1], landed, n_hubs - 1)
+        drain(recv_sems.at[2], landed, n_hubs - 1)
 
     @pl.when(jnp.logical_not(is_hub))
     def _():
-        drain(recv_sems.at[1], landed, n_hubs)
+        drain(recv_sems.at[2], landed, n_hubs)
 
     prior = jnp.concatenate(split(landed[...].reshape(width, width)), axis=0)
 
     def finish(piece, ahead):
-        for j in range(per_piece):
-            part = rows((piece * per_piece + j) * BLOCK, BLOCK)
+        for j in range(blocks // 2):
+            part = rows((piece * (blocks // 2) + j) * BLOCK, BLOCK)
             queries = q[part, :]
             inter = jnp.dot(
                 jnp.concatenate([queries, queries], axis=1), prior, preferred_element_type=F32
@@ -242,7 +272,7 @@
             ahead = ahead * decay
         return ahead
 
-    lax.fori_loop(0, PIECES, finish, ones)
+    lax.fori_loop(0, 2, finish, ones)
 
     @pl.when(is_hub)
     def _():
@@ -251,25 +281,42 @@
 
         @pl.when(2 * chip == me)
         def _():
-            drain(send_sems.at[2], finals.at[pl.ds(0, n_head - 1)], n_head - 1)
+            drain(send_sems.at[2], finals, n_head - 1)
 
         @pl.when(2 * chip != me)
         def _():
             drain(send_sems.at[2], finals, n_head)
 
-        drain(send_sems.at[2], finals, n_head)
+        @pl.when(skip)
+        def _():
+            drain(send_sems.at[2], finals, n_head - 1)
+
+        @pl.when(jnp.logical_not(skip))
+        def _():
+            drain(send_sems.at[2], finals, n_head)
 
     @pl.when(jnp.logical_not(is_hub))
     def _():
         drain(send_sems.at[0], own, n_hubs)
 
-    @pl.when(my_hub == me)
-    def _():
-        drain(recv_sems.at[2], finals, n_head - 1)
-
-    @pl.when(my_hub != me)
-    def _():
-        drain(recv_sems.at[2], finals, n_head)
+    @pl.when(is_far)
+    def _():
+        to_early.wait_send()
+
+    @pl.when(is_early)
+    def _():
+        drain(recv_sems.at[3], finals, far)
+        pltpu.make_async_copy(direct, direct, recv_sems.at[4]).wait()
+        for head in range(far, n_head):
+            finals[head] = jnp.sum(direct[head - far], axis=0)
+
+    @pl.when(jnp.logical_and(my_hub == me, jnp.logical_not(is_early)))
+    def _():
+        drain(recv_sems.at[3], finals, n_head - 1)
+
+    @pl.when(jnp.logical_and(my_hub != me, jnp.logical_not(is_early)))
+    def _():
+        drain(recv_sems.at[3], finals, n_head)
 
     final[...] = finals[...]
 
@@ -319,10 +366,12 @@
             pltpu.VMEM((n_hubs, 2 * share, width), F32),
             pltpu.VMEM((2, share, width), F32),
             pltpu.VMEM((n_head, share, width), F32),
+            pltpu.VMEM((share, width), F32),
+            pltpu.VMEM((n_head - n_head // 2, n_seq, share, width), F32),
             pltpu.SemaphoreType.DMA((3, PIECES)),
             pltpu.SemaphoreType.DMA((2,)),
-            pltpu.SemaphoreType.DMA((3,)),
-            pltpu.SemaphoreType.DMA((3,)),
+            pltpu.SemaphoreType.DMA((4,)),
+            pltpu.SemaphoreType.DMA((5,)),
             pltpu.SemaphoreType.REGULAR,
         ],
         compiler_params=pltpu.CompilerParams(

time: 22.8 us -> 21.1 us (0.925)
  the two profiles are of different devices: /device:TPU:1 before, /device:TPU:6 now
where the time goes in v3:
time: 21.1 us; the launch traced here: 21 us
  Pallas kernels  19.7 us (93%)
  between operations  1.29 us (6%)
    pallas_call x1, Pallas kernels, on_device(): pl.pallas_call(functools.partial(state_kernel, n_seq, n_head), out_shape=...  18.3 us
    pallas_call x1, Pallas kernels, on_device(): pl.pallas_call(write_kernel, out_shape=(jax.ShapeDtypeStruct((tokens, wid...  1.36 us

profile of v3, /device:TPU:6, one launch (start us, length us, event | category | flops | bytes accessed | tf_op | source)
XLA Modules:
  0.0 21.0 jit_solution(2087951244468767509)
XLA Ops:
  1.3 18.3 %state.1 = (bf16[8192,128]{1,0:T(8,128)(2,1)S(1)}, f32[8,4,128]{2,1,0:T(4,128)S(1)}) custom-call(s32[1]{0:T(128)S(6)} %copy.7.exps_hbm, f32[1,128]{1,0:T(1,128)} %bitcast.1, bf16[8192,128]{1,0:T(8,128)(2,1)} %q_hbm.1, bf16[8192,128]{1,0:T(8,128)(2,1)} %k_hbm.1, bf16[8192,128]{1,0:T(8,128)(2,1)} %v_hbm.1), custom_call_target="tpu_custom_call" | custom-call | tf_op jit(solution)/shard_map/state/pallas_call | solution.py:344
  19.6 1.4 %write.1 = (bf16[8192,128]{1,0:T(8,128)(2,1)}, f32[8,4,128]{2,1,0:T(4,128)}) custom-call(bf16[8192,128]{1,0:T(8,128)(2,1)S(1)} %get-tuple-element.4.out, f32[8,4,128]{2,1,0:T(4,128)S(1)} %get-tuple-element.5.final), custom_call_target="tpu_custom_call" | custom-call | tf_op jit(solution)/shard_map/write/pallas_call | solution.py:385

commit v4 on v3

v4 whole, which is shorter than its diff:
```python
import functools

import jax
import jax.numpy as jnp
from jax import lax
from jax.experimental import pallas as pl
from jax.experimental.pallas import tpu as pltpu
from jax.sharding import PartitionSpec as P

BLOCK = 256
PIECES = 4
EARLY = 1
TURN = 2
MESH = pl.DeviceIdType.MESH
F32 = jnp.float32
BF16 = jnp.bfloat16


def hub_chips(chips):
    if chips == 16:
        return ((0, 7), (1, 6), (2, 14), (3, 11), (4, 9), (5, 10), (8, 13), (12, 15))
    return tuple((chip, chips - 1 - chip) for chip in range(chips // 2))


def pick(index, table):
    value = jnp.int32(table[0])
    for entry in range(1, len(table)):
        value = jnp.where(index == entry, jnp.int32(table[entry]), value)
    return value


def rows(start, count):
    return pl.ds(pl.multiple_of(start, count), count)


def split(value):
    high = value.astype(BF16)
    return high, (value - high.astype(F32)).astype(BF16)


def state_kernel(
    n_seq, n_head,
    exps_hbm, gain_hbm, q_hbm, k_hbm, v_hbm,
    out, final,
    q, k, v, raw, exps, gain, within, lead, tail, before, own, gathered, prefix, landed,
    last, finals, toward, direct, in_sems, small_sems, send_sems, recv_sems, ready,
):
    me, mine = lax.axis_index("seq"), lax.axis_index("head")
    n_hubs = n_seq // 4
    tokens, width = q.shape
    blocks = tokens // BLOCK
    cuts = [blocks * part // 16 for part in (0, 5, 10, 14, 16)]
    share = width // n_seq
    def load(which, piece):
        src, dst = ((k_hbm, k), (v_hbm, v))[which]
        part = pl.ds(cuts[piece] * BLOCK, (cuts[piece + 1] - cuts[piece]) * BLOCK)
        return pltpu.make_async_copy(src.at[part], dst.at[part], in_sems.at[which, piece])

    read_exps = pltpu.make_async_copy(exps_hbm, exps, small_sems.at[0])
    read_q = pltpu.make_async_copy(q_hbm, q, in_sems.at[2, 0])
    read_gain = pltpu.make_async_copy(gain_hbm, gain, small_sems.at[1])
    read_exps.start()
    for piece in range(PIECES):
        load(0, piece).start()
        load(1, piece).start()
    read_gain.start()

    seats = hub_chips(2 * n_hubs)
    seat_spots = {chip: spot for spot, pair in enumerate(seats) for chip in pair}
    my_spot = pick(me // 2, [seat_spots[chip] for chip in range(2 * n_hubs)])
    other = pick(my_spot, [pair[1] for pair in seats])
    home = 2 * pick(my_spot, [pair[0] for pair in seats]) + 1
    core = lax.rem(me, 2)
    targets = (me, 2 * (me // 2) + 1 - core, 2 * other + 1, 2 * other)

    def hub(first, head):
        return first - jnp.logical_and(first == EARLY, head == 0).astype(jnp.int32)

    is_hub = hub(home, mine) == me
    hub_count = is_hub.astype(jnp.int32)
    far = n_head // 2
    is_far = mine >= far
    skip = jnp.logical_and(me == EARLY, is_far)
    is_early = jnp.logical_and(me == EARLY, mine == 0)
    quarter = n_seq // 4

    barrier = pltpu.get_barrier_semaphore()

    def signal(sem, seq, head):
        pl.semaphore_signal(
            sem, inc=1, device_id={"seq": seq, "head": head}, device_id_type=MESH
        )

    @pl.when(is_hub)
    def _():
        @pl.loop(0, n_seq)
        def _(step):
            to = n_seq - 1 - step

            @pl.when(to != me)
            def _():
                signal(barrier, to, mine)

        @pl.loop(mine + 1, n_head)
        def _(head):
            for target in targets:
                signal(barrier, target, head)

    @pl.loop(mine + 1, n_head)
    def _(head):
        signal(barrier, hub(home, head), head)

    @pl.when(is_early)
    def _():
        @pl.loop(far, n_head)
        def _(head):
            @pl.loop(0, n_seq)
            def _(seq):
                signal(barrier, seq, head)

    read_exps.wait()
    rate = exps[0].astype(F32) / 16777216.0
    row = lax.broadcasted_iota(jnp.int32, (BLOCK, width), 0).astype(F32)
    tail[...] = jnp.exp2(-rate * (BLOCK - 1.0 - row))
    ones = jnp.ones((1, width), F32)
    decay = jnp.exp2(-rate * BLOCK * ones)
    whole = jnp.exp2(-rate * tokens * ones)

    total = jnp.zeros((width, width), F32)
    for piece in range(PIECES):
        load(0, piece).wait()
        load(1, piece).wait()
        if piece == PIECES - 1:
            read_q.start()
        for block in range(cuts[piece], cuts[piece + 1]):
            part = pl.ds(block * BLOCK, BLOCK)
            scaled = (k[part, :].astype(F32) * tail[...]).astype(BF16)
            term = lax.dot_general(
                scaled, v[part, :], (((0,), (0,)), ((), ())), preferred_element_type=F32
            )
            before[block] = total
            total = total * decay + term
    for spot in range(n_hubs):
        for slot, seat in enumerate(seats[spot]):
            own[spot, 2 * share * slot:2 * share * (slot + 1), :] = (
                total[2 * share * seat:2 * share * (seat + 1), :]
            )
    left = (n_seq - 1 - me).astype(F32) * tokens
    toward[...] = total[EARLY * share:(EARLY + 1) * share, :] * jnp.exp2(-rate * left * ones)

    pl.semaphore_wait(
        barrier, n_hubs - hub_count + mine * (1 + 4 * hub_count) + is_far.astype(jnp.int32)
    )

    def contribution(to, spot):
        return pltpu.make_async_remote_copy(
            src_ref=own.at[spot], dst_ref=gathered.at[me], send_sem=send_sems.at[0],
            recv_sem=recv_sems.at[me // quarter], device_id={"seq": to, "head": mine}, device_id_type=MESH,
        )

    def entering(to):
        return pltpu.make_async_remote_copy(
            src_ref=prefix.at[to], dst_ref=landed.at[my_spot], send_sem=send_sems.at[1],
            recv_sem=recv_sems.at[4], device_id={"seq": to, "head": mine}, device_id_type=MESH,
        )

    def ending(which, head):
        return pltpu.make_async_remote_copy(
            src_ref=last.at[which], dst_ref=finals.at[mine], send_sem=send_sems.at[2],
            recv_sem=recv_sems.at[5], device_id={"seq": targets[which], "head": head},
            device_id_type=MESH,
        )

    to_early = pltpu.make_async_remote_copy(
        src_ref=toward, dst_ref=direct.at[jnp.maximum(mine - far, 0), me], send_sem=send_sems.at[3],
        recv_sem=recv_sems.at[6], device_id={"seq": EARLY, "head": 0}, device_id_type=MESH,
    )

    @pl.when(is_far)
    def _():
        to_early.start()

    def drain(sem, ref, count):
        part = ref.at[pl.ds(0, count)]
        pltpu.make_async_copy(part, part, sem).wait()

    def contribute(order):
        for spot in order:
            to = hub(jnp.int32(2 * seats[spot][0] + 1), mine)

            @pl.when(me != to)
            def _():
                contribution(to, spot).start()

    order = list(range(n_hubs))

    @pl.when(lax.rem(me // 2, 2) == 0)
    def _():
        contribute(order)

    @pl.when(lax.rem(me // 2, 2) == 1)
    def _():
        contribute(order[n_hubs // 2:] + order[:n_hubs // 2])

    @pl.loop(0, mine)
    def _(head):
        signal(ready, hub(home, head), head)

    lead[...] = jnp.exp2(-rate * (row + 1.0))
    gap = (
        lax.broadcasted_iota(jnp.int32, (BLOCK, BLOCK), 0)
        - lax.broadcasted_iota(jnp.int32, (BLOCK, BLOCK), 1)
    ).astype(F32)
    within[...] = jnp.where(gap >= 0.0, jnp.exp2(-rate * jnp.maximum(gap, 0.0)), 0.0)

    def attend(block, carry):
        part = rows(block * BLOCK, BLOCK)
        queries, vals = q[part, :], v[part, :]
        scores = lax.dot_general(
            queries, k[part, :], (((1,), (1,)), ((), ())), preferred_element_type=F32
        )
        weights = (scores * within[...]).astype(BF16)
        local = jnp.dot(weights, vals, preferred_element_type=F32)
        inter = jnp.dot(
            jnp.concatenate([queries, queries], axis=1),
            jnp.concatenate(split(before[block]), axis=0),
            preferred_element_type=F32,
        )
        raw[part, :] = local + lead[...] * inter
        return carry

    read_q.wait()
    groups = 4
    group_blocks = blocks // groups

    duty = jnp.where(is_far, TURN, groups)

    @pl.loop(0, groups + 1)
    def _(group):
        @pl.when(jnp.logical_and(is_hub, group == duty))
        def _():
            gathered[me] = own[my_spot]
            state = jnp.zeros(gathered.shape[1:], F32)
            for step in range(n_seq):
                if step % quarter == 0:
                    group_sem = recv_sems.at[step // quarter]

                    @pl.when(me // quarter != step // quarter)
                    def _():
                        drain(group_sem, gathered, quarter)

                    if quarter > 1:
                        @pl.when(me // quarter == step // quarter)
                        def _():
                            drain(group_sem, gathered, quarter - 1)

                prefix[step] = state
                state = state * whole + gathered[step]
            lower, upper = state[:share, :], state[share:2 * share, :]
            last[0] = jnp.where(core == 1, upper, lower)
            last[1] = jnp.where(core == 1, lower, upper)
            last[2] = state[3 * share:, :]
            last[3] = state[2 * share:3 * share, :]

            @pl.loop(0, jnp.minimum(mine, far))
            def _(head):
                @pl.when(jnp.logical_not(jnp.logical_and(skip, head == 0)))
                def _():
                    ending(0, head).start()

                for which in (1, 2, 3):
                    ending(which, head).start()

            landed[my_spot] = prefix[me]

            for start in (n_seq // 2, 0):
                @pl.loop(0, n_seq // 2)
                def _(step):
                    to = start + lax.rem(me + step, n_seq // 2)

                    @pl.when(to != me)
                    def _():
                        entering(to).start()

            finals[mine] = last[0]
            for which in (1, 2, 3):
                ending(which, mine).start()

            @pl.loop(far, mine)
            def _(head):
                for which in range(4):
                    ending(which, head).start()

            @pl.when(mine < n_head - 1)
            def _():
                pl.semaphore_wait(ready, 4 * (n_head - 1 - mine))

            @pl.loop(mine + 1, n_head)
            def _(head):
                for which in range(4):
                    ending(which, head).start()

        @pl.when(group < groups)
        def _():
            for j in range(group_blocks):
                attend(group * group_blocks + j, 0)

    read_gain.wait()

    @pl.when(is_hub)
    def _():
        if n_hubs > 1:
            drain(recv_sems.at[4], landed, n_hubs - 1)

    @pl.when(jnp.logical_not(is_hub))
    def _():
        drain(recv_sems.at[4], landed, n_hubs)

    parts = [None] * (2 * n_hubs)
    for spot in range(n_hubs):
        for slot, seat in enumerate(seats[spot]):
            parts[seat] = landed[spot, 2 * share * slot:2 * share * (slot + 1), :]
    prior = jnp.concatenate(split(jnp.concatenate(parts, axis=0)), axis=0)

    def finish(piece, ahead):
        for j in range(blocks // 2):
            part = rows((piece * (blocks // 2) + j) * BLOCK, BLOCK)
            queries = q[part, :]
            inter = jnp.dot(
                jnp.concatenate([queries, queries], axis=1), prior, preferred_element_type=F32
            )
            value = raw[part, :] + (lead[...] * ahead) * inter
            mean_sq = jnp.mean(value * value, axis=-1, keepdims=True)
            out[part, :] = (value * lax.rsqrt(mean_sq + 1e-06) * gain[...]).astype(BF16)
            ahead = ahead * decay
        return ahead

    lax.fori_loop(0, 2, finish, ones)

    @pl.when(is_hub)
    def _():
        if n_hubs > 1:
            drain(send_sems.at[0], own, n_hubs - 1)
        drain(send_sems.at[1], prefix, n_seq - 1)
        for _ in range(3):
            drain(send_sems.at[2], finals, n_head)

        @pl.when(skip)
        def _():
            if n_head > 2:
                drain(send_sems.at[2], finals, n_head - 2)

        @pl.when(jnp.logical_not(skip))
        def _():
            drain(send_sems.at[2], finals, n_head - 1)

    @pl.when(jnp.logical_not(is_hub))
    def _():
        drain(send_sems.at[0], own, n_hubs)

    @pl.when(is_far)
    def _():
        to_early.wait_send()

    @pl.when(is_early)
    def _():
        drain(recv_sems.at[5], finals, far)
        pltpu.make_async_copy(direct, direct, recv_sems.at[6]).wait()
        for head in range(far, n_head):
            finals[head] = jnp.sum(direct[head - far], axis=0)

    @pl.when(jnp.logical_and(is_hub, jnp.logical_not(is_early)))
    def _():
        drain(recv_sems.at[5], finals, n_head - 1)

    @pl.when(jnp.logical_not(jnp.logical_or(is_hub, is_early)))
    def _():
        drain(recv_sems.at[5], finals, n_head)

    final[...] = finals[...]


def write_kernel(out, final, out_hbm, final_hbm, sems):
    piece_rows = out.shape[0] // PIECES
    copies = [pltpu.make_async_copy(final, final_hbm, sems.at[PIECES])]
    for piece in range(PIECES):
        part = pl.ds(piece * piece_rows, piece_rows)
        copies.append(pltpu.make_async_copy(out.at[part], out_hbm.at[part], sems.at[piece]))
    for copy in copies:
        copy.start()
    for copy in copies:
        copy.wait()


def on_device(n_seq, n_head, queries, keys, values, exponents, gain):
    tokens, width = queries.shape
    share = width // n_seq
    n_hubs = n_seq // 4
    vmem = pl.BlockSpec(memory_space=pltpu.VMEM)
    anywhere = pl.BlockSpec(memory_space=pl.ANY)
    hbm = pl.BlockSpec(memory_space=pltpu.HBM)
    blocks = tokens // BLOCK
    kept = pl.pallas_call(
        functools.partial(state_kernel, n_seq, n_head),
        out_shape=(
            pltpu.VMEM((tokens, width), BF16),
            pltpu.VMEM((n_head, share, width), F32),
        ),
        in_specs=[anywhere] + [hbm] * 4,
        out_specs=(vmem,) * 2,
        scratch_shapes=[
            pltpu.VMEM((tokens, width), BF16),
            pltpu.VMEM((tokens, width), BF16),
            pltpu.VMEM((tokens, width), BF16),
            pltpu.VMEM((tokens, width), F32),
            pltpu.SMEM((1,), jnp.int32),
            pltpu.VMEM((1, width), F32),
            pltpu.VMEM((BLOCK, BLOCK), F32),
            pltpu.VMEM((BLOCK, width), F32),
            pltpu.VMEM((BLOCK, width), F32),
            pltpu.VMEM((blocks, width, width), F32),
            pltpu.VMEM((n_hubs, 4 * share, width), F32),
            pltpu.VMEM((n_seq, 4 * share, width), F32),
            pltpu.VMEM((n_seq, 4 * share, width), F32),
            pltpu.VMEM((n_hubs, 4 * share, width), F32),
            pltpu.VMEM((4, share, width), F32),
            pltpu.VMEM((n_head, share, width), F32),
            pltpu.VMEM((share, width), F32),
            pltpu.VMEM((n_head - n_head // 2, n_seq, share, width), F32),
            pltpu.SemaphoreType.DMA((3, PIECES)),
            pltpu.SemaphoreType.DMA((2,)),
            pltpu.SemaphoreType.DMA((4,)),
            pltpu.SemaphoreType.DMA((7,)),
            pltpu.SemaphoreType.REGULAR,
        ],
        compiler_params=pltpu.CompilerParams(
            collective_id=0, has_side_effects=True, vmem_limit_bytes=40 * 1024 * 1024
        ),
        name="state",
    )(exponents, *(
        pltpu.with_memory_space_constraint(array, pltpu.HBM)
        for array in (gain.reshape(1, width), queries, keys, values)
    ))
    return pl.pallas_call(
        write_kernel,
        out_shape=(
            jax.ShapeDtypeStruct((tokens, width), BF16),
            jax.ShapeDtypeStruct((n_head, share, width), F32),
        ),
        in_specs=[vmem] * 2,
        out_specs=(anywhere, anywhere),
        scratch_shapes=[pltpu.SemaphoreType.DMA((PIECES + 1,))],
        compiler_params=pltpu.CompilerParams(vmem_limit_bytes=32 * 1024 * 1024),
        name="write",
    )(*kept)


def solution(mesh):
    return jax.shard_map(
        functools.partial(on_device, mesh.shape["seq"], mesh.shape["head"]),
        mesh=mesh,
        in_specs=(P("seq", "head"), P("seq", "head"), P("seq", "head"), P("head"), P("head")),
        out_specs=(P("seq", "head"), P(None, "seq", None)),
        check_vma=False,
    )
```

time: 21.1 us -> 20.6 us (0.976)
  the two profiles are of different devices: /device:TPU:6 before, /device:TPU:1 now
where the time goes in v4:
time: 20.6 us; the launch traced here: 20.3 us
  Pallas kernels  19 us (92%)
  between operations  1.29 us (6%)
    pallas_call x1, Pallas kernels, on_device(): pl.pallas_call(functools.partial(state_kernel, n_seq, n_head), out_shape=...  17.6 us
    pallas_call x1, Pallas kernels, on_device(): pl.pallas_call(write_kernel, out_shape=(jax.ShapeDtypeStruct((tokens, wid...  1.36 us

profile of v4, /device:TPU:1, one launch (start us, length us, event | category | flops | bytes accessed | tf_op | source)
XLA Modules:
  0.0 20.3 jit_solution(6135360895140153404)
XLA Ops:
  1.3 17.6 %state.1 = (bf16[8192,128]{1,0:T(8,128)(2,1)S(1)}, f32[8,4,128]{2,1,0:T(4,128)S(1)}) custom-call(s32[1]{0:T(128)S(6)} %copy.7.exps_hbm, f32[1,128]{1,0:T(1,128)} %bitcast.1, bf16[8192,128]{1,0:T(8,128)(2,1)} %q_hbm.1, bf16[8192,128]{1,0:T(8,128)(2,1)} %k_hbm.1, bf16[8192,128]{1,0:T(8,128)(2,1)} %v_hbm.1), custom_call_target="tpu_custom_call" | custom-call | tf_op jit(solution)/shard_map/state/pallas_call | solution.py:403
  18.9 1.4 %write.1 = (bf16[8192,128]{1,0:T(8,128)(2,1)}, f32[8,4,128]{2,1,0:T(4,128)}) custom-call(bf16[8192,128]{1,0:T(8,128)(2,1)S(1)} %get-tuple-element.4.out, f32[8,4,128]{2,1,0:T(4,128)S(1)} %get-tuple-element.5.final), custom_call_target="tpu_custom_call" | custom-call | tf_op jit(solution)/shard_map/write/pallas_call | solution.py:444

commit v5 on v4

--- a/solution.py
+++ b/solution.py
@@ -8,8 +8,9 @@
 from jax.sharding import PartitionSpec as P
 
 BLOCK = 256
-PIECES = 4
+PIECES = 2
 EARLY = 1
+URGENT = (0, 1, 4, 6)
 TURN = 2
 MESH = pl.DeviceIdType.MESH
 F32 = jnp.float32
@@ -49,11 +50,11 @@
     n_hubs = n_seq // 4
     tokens, width = q.shape
     blocks = tokens // BLOCK
-    cuts = [blocks * part // 16 for part in (0, 5, 10, 14, 16)]
+    per_piece = blocks // PIECES
     share = width // n_seq
     def load(which, piece):
         src, dst = ((k_hbm, k), (v_hbm, v))[which]
-        part = pl.ds(cuts[piece] * BLOCK, (cuts[piece + 1] - cuts[piece]) * BLOCK)
+        part = rows(piece * per_piece * BLOCK, per_piece * BLOCK)
         return pltpu.make_async_copy(src.at[part], dst.at[part], in_sems.at[which, piece])
 
     read_exps = pltpu.make_async_copy(exps_hbm, exps, small_sems.at[0])
@@ -126,20 +127,22 @@
     decay = jnp.exp2(-rate * BLOCK * ones)
     whole = jnp.exp2(-rate * tokens * ones)
 
-    total = jnp.zeros((width, width), F32)
-    for piece in range(PIECES):
+    def add(piece, total):
         load(0, piece).wait()
         load(1, piece).wait()
-        if piece == PIECES - 1:
-            read_q.start()
-        for block in range(cuts[piece], cuts[piece + 1]):
-            part = pl.ds(block * BLOCK, BLOCK)
+        for j in range(per_piece):
+            block = piece * per_piece + j
+            part = rows(block * BLOCK, BLOCK)
             scaled = (k[part, :].astype(F32) * tail[...]).astype(BF16)
             term = lax.dot_general(
                 scaled, v[part, :], (((0,), (0,)), ((), ())), preferred_element_type=F32
             )
             before[block] = total
             total = total * decay + term
+        return total
+
+    total = lax.fori_loop(0, PIECES, add, jnp.zeros((width, width), F32))
+    read_q.start()
     for spot in range(n_hubs):
         for slot, seat in enumerate(seats[spot]):
             own[spot, 2 * share * slot:2 * share * (slot + 1), :] = (
@@ -192,15 +195,7 @@
             def _():
                 contribution(to, spot).start()
 
-    order = list(range(n_hubs))
-
-    @pl.when(lax.rem(me // 2, 2) == 0)
-    def _():
-        contribute(order)
-
-    @pl.when(lax.rem(me // 2, 2) == 1)
-    def _():
-        contribute(order[n_hubs // 2:] + order[:n_hubs // 2])
+    contribute(sorted(range(n_hubs), key=lambda spot: URGENT.index(spot) if spot in URGENT else n_hubs))
 
     @pl.loop(0, mine)
     def _(head):
@@ -381,9 +376,9 @@
 
 
 def write_kernel(out, final, out_hbm, final_hbm, sems):
-    piece_rows = out.shape[0] // PIECES
-    copies = [pltpu.make_async_copy(final, final_hbm, sems.at[PIECES])]
-    for piece in range(PIECES):
+    piece_rows = out.shape[0] // 4
+    copies = [pltpu.make_async_copy(final, final_hbm, sems.at[4])]
+    for piece in range(4):
         part = pl.ds(piece * piece_rows, piece_rows)
         copies.append(pltpu.make_async_copy(out.at[part], out_hbm.at[part], sems.at[piece]))
     for copy in copies:
@@ -449,7 +444,7 @@
         ),
         in_specs=[vmem] * 2,
         out_specs=(anywhere, anywhere),
-        scratch_shapes=[pltpu.SemaphoreType.DMA((PIECES + 1,))],
+        scratch_shapes=[pltpu.SemaphoreType.DMA((5,))],
         compiler_params=pltpu.CompilerParams(vmem_limit_bytes=32 * 1024 * 1024),
         name="write",
     )(*kept)

time: 20.6 us -> 20.6 us (level)
  no operation moved by 1% of the time
where the time goes in v5:
time: 20.6 us; the launch traced here: 20.2 us
  Pallas kernels  19 us (92%)
  between operations  1.29 us (6%)
    pallas_call x1, Pallas kernels, on_device(): pl.pallas_call(functools.partial(state_kernel, n_seq, n_head), out_shape=...  17.6 us
    pallas_call x1, Pallas kernels, on_device(): pl.pallas_call(write_kernel, out_shape=(jax.ShapeDtypeStruct((tokens, wid...  1.36 us

profile of v5, /device:TPU:1, one launch (start us, length us, event | category | flops | bytes accessed | tf_op | source)
XLA Modules:
  0.0 20.2 jit_solution(10900207865847866243)
XLA Ops:
  1.3 17.6 %state.1 = (bf16[8192,128]{1,0:T(8,128)(2,1)S(1)}, f32[8,4,128]{2,1,0:T(4,128)S(1)}) custom-call(s32[1]{0:T(128)S(6)} %copy.7.exps_hbm, f32[1,128]{1,0:T(1,128)} %bitcast.1, bf16[8192,128]{1,0:T(8,128)(2,1)} %q_hbm.1, bf16[8192,128]{1,0:T(8,128)(2,1)} %k_hbm.1, bf16[8192,128]{1,0:T(8,128)(2,1)} %v_hbm.1), custom_call_target="tpu_custom_call" | custom-call | tf_op jit(solution)/shard_map/state/pallas_call | solution.py:398
  18.9 1.4 %write.1 = (bf16[8192,128]{1,0:T(8,128)(2,1)}, f32[8,4,128]{2,1,0:T(4,128)}) custom-call(bf16[8192,128]{1,0:T(8,128)(2,1)S(1)} %get-tuple-element.4.out, f32[8,4,128]{2,1,0:T(4,128)S(1)} %get-tuple-element.5.final), custom_call_target="tpu_custom_call" | custom-call | tf_op jit(solution)/shard_map/write/pallas_call | solution.py:439
